TPU v7x, 32 devices: a whole 2x2x4 slice. The times are simulated.
32 devices in a mesh: sec: 4 (over x, core), op: 8 (over z, y).
Axes of the slice: x: 2, y: 2, z: 4, core: 2. Of those that a mesh axis runs over, the one named last changes fastest.
Arguments:
- psi_blocks: bfloat16 [1536, 384], P('sec'), may hold values from -0.078125 to 0.078125
- sector_rows: int32 [4], P('sec'), may hold values from 96 to 384, as said below
- kept_cols: int32 [4], P('sec'), may hold values from 96 to 384, as said below
- basis: bfloat16 [1536, 384], P('sec'), may hold values from -0.3125 to 0.3125
- left_ops: bfloat16 [16, 1536, 1152], P('op', 'sec'), may hold values from -6 to 6
- right_ops: bfloat16 [16, 4, 3, 384, 384], P('op', 'sec'), may hold values from -0.1875 to 0.1875
Outputs:
- sigma: bfloat16 [1536, 384], P(('sec', 'op'))
- renorm_ops: bfloat16 [16, 1536, 1152], P(None, ('sec', 'op'))
Inputs may be any that keep to these rules, and one draw needn't show every extreme that they name: `sector_rows`: some sector has exactly 384 live states and another exactly 96. `kept_cols`: some sector keeps exactly 384 states and another exactly 96.
All inputs are finite; a program needn't handle non-finite values.
Results may differ from a plain program's by a relative error of at most 0.0049.
Values may be sent and summed in bfloat16 or wider, within the bound.
A program may use at most 64 MiB of HBM per device.

v0:
```python
import jax
import jax.numpy as jnp
from jax import lax
from jax.sharding import PartitionSpec as P


def padded(block, sides, width):
    for axis, dim in sides:
        count = lax.axis_size(axis)
        forward = [(i, i + 1) for i in range(count - 1)]
        backward = [(target, source) for source, target in forward]
        low = lax.ppermute(
            lax.slice_in_dim(block, block.shape[dim] - width, None, axis=dim), axis, forward
        )
        high = lax.ppermute(lax.slice_in_dim(block, 0, width, axis=dim), axis, backward)
        block = jnp.concatenate([low, block, high], axis=dim)
    return block


def local(psi_blocks, sector_rows, kept_cols, basis, left_ops, right_ops):
    row_count = psi_blocks.shape[0]
    state_width = psi_blocks.shape[1]
    kept_width = basis.shape[1]
    live_rows = jnp.arange(row_count, dtype=jnp.int32) < sector_rows[0]
    live_columns = jnp.arange(kept_width, dtype=jnp.int32) < kept_cols[0]
    psi_live = jnp.where(live_rows[:, None], psi_blocks, jnp.zeros((), jnp.bfloat16))
    basis_live = jnp.where(
        live_rows[:, None] & live_columns[None, :], basis, jnp.zeros((), jnp.bfloat16)
    )
    joined = jnp.concatenate([psi_live, basis_live], axis=1)
    extended = padded(joined, (("sec", 0),), row_count)
    near_state = extended[:, :state_width]
    near_basis = extended[:, state_width:]
    right_part = right_ops[:, 0]
    accumulated = jnp.zeros((row_count, state_width), jnp.float32)
    for sigma_neighbor in range(3):
        left_part = left_ops[:, :, sigma_neighbor * row_count : (sigma_neighbor + 1) * row_count]
        product = jnp.einsum(
            "krs,sn->krn",
            left_part,
            near_state[sigma_neighbor * row_count : (sigma_neighbor + 1) * row_count],
            preferred_element_type=jnp.float32,
        ).astype(jnp.bfloat16)
        accumulated = accumulated + jnp.einsum(
            "krn,kmn->rm",
            product,
            right_part[:, sigma_neighbor],
            preferred_element_type=jnp.float32,
        )
    sigma = lax.psum_scatter(
        jnp.where(live_rows[:, None], accumulated, jnp.float32(0.0)),
        "op",
        scatter_dimension=0,
        tiled=True,
    )

    def renorm_piece(neighbor):
        left_part = left_ops[:, :, neighbor * row_count : (neighbor + 1) * row_count]
        vmatrix = jnp.einsum(
            "krs,sc->krc",
            left_part,
            near_basis[neighbor * row_count : (neighbor + 1) * row_count],
            preferred_element_type=jnp.float32,
        ).astype(jnp.bfloat16)
        return jnp.einsum(
            "rc,krq->kcq", basis_live, vmatrix, preferred_element_type=jnp.float32
        ).astype(jnp.bfloat16)

    renorm_local = jnp.concatenate([renorm_piece(neighbor) for neighbor in range(3)], axis=2)
    renorm_ops = lax.all_to_all(renorm_local, "op", split_axis=1, concat_axis=0, tiled=True)
    return (sigma.astype(jnp.bfloat16), renorm_ops)


def solution(mesh):
    placed = (
        P("sec", None),
        P("sec"),
        P("sec"),
        P("sec", None),
        P("op", "sec", None),
        P("op", "sec", None, None, None),
    )
    return jax.shard_map(
        local,
        mesh=mesh,
        in_specs=placed,
        out_specs=(P(("sec", "op"), None), P(None, ("sec", "op"), None)),
        check_vma=False,
    )
```

profile of v0, /device:TPU:0, one launch (start us, length us, event | category | flops | bytes accessed | tf_op | source)
XLA Modules:
  0.0 131.3 jit_solution(14718643599512853776)
XLA Ops:
  7.2 1.2 copy.27
  9.6 1.2 copy.28
  10.8 0.2 broadcast_select_fusion
  11.1 0.7 copy-done.2
  11.7 0.1 pad_maximum_fusion.1
  11.8 1.3 collective-permute-start.1
  13.1 3.1 %collective-permute-start = (bf16[384,768]{0,1:T(8,128)(2,1)S(1)}, bf16[384,768]{0,1:T(8,128)(2,1)S(1)}, u32[]{:S(2)}, u32[]{:S(2)}) collective-permute-start(bf16[384,768]{0,1:T(8,128)(2,1)S(1)} %pad_maximum_fusion.1), channel_id=1, source_target_pairs={{0,8},{8,16},{16,24},{1,9},{9,17},{17,25},{2,10},{10,18},{18,26},{... | collective-permute-start | bytes 1769480 | tf_op jit(solution)/shard_map/ppermute | solution.py:12
  16.2 2.0 %fusion.6 = bf16[2,384,384]{1,2,0:T(8,128)(2,1)S(1)} fusion(bf16[2,384,1152]{2,1,0:T(8,128)(2,1)} %param.10, bf16[384,384]{0,1:T(8,128)(2,1)S(1)} %get-tuple-element.7), kind=kOutput, calls=%fused_computation.20 | convolution fusion | flops 453574656 | bytes 1769472 | tf_op jit(solution)/shard_map/rc,krq->kcq/dot_general | solution.py:65
  18.3 2.3 %fusion.8 = bf16[2,384,384]{1,2,0:T(8,128)(2,1)S(1)} fusion(bf16[2,384,1152]{2,1,0:T(8,128)(2,1)} %param.10, bf16[384,768]{0,1:T(8,128)(2,1)S(1)} %collective-permute-done.1, bf16[384,384]{0,1:T(8,128)(2,1)S(1)} %get-tuple-element.7), kind=kOutput, calls=%fused_computation.22 | convolution fusion | flops 453574656 | bytes 1769472 | tf_op jit(solution)/shard_map/rc,krq->kcq/dot_general | solution.py:65
  20.5 0.8 copy-done.4
  21.4 2.0 %fusion.4 = bf16[2,384,384]{1,2,0:T(8,128)(2,1)S(1)} fusion(bf16[2,384,1152]{2,1,0:T(8,128)(2,1)} %param.10, bf16[384,768]{0,1:T(8,128)(2,1)S(1)} %collective-permute-done, bf16[384,384]{0,1:T(8,128)(2,1)S(1)} %get-tuple-element.7), kind=kOutput, calls=%fused_computation.18 | convolution fusion | flops 453574656 | bytes 1769472 | tf_op jit(solution)/shard_map/rc,krq->kcq/dot_general | solution.py:65
  23.4 0.2 pad_maximum_fusion
  23.6 4.5 %copy.39 = bf16[2,384,1152]{2,0,1:T(2,128)(2,1)} copy(bf16[2,384,1152]{1,2,0:T(8,128)(2,1)S(1)} %pad_maximum_fusion) | data formatting | bytes 3538944 | tf_op jit(solution)/shard_map/concatenate | solution.py:69
  28.1 7.4 %all-to-all-start = ((bf16[2,384,1152]{2,0,1:T(2,128)(2,1)}), bf16[2,384,1152]{2,0,1:T(2,128)(2,1)S(1)}, u32[]{:S(2)}, u32[]{:S(2)}) async-start(bf16[2,384,1152]{2,0,1:T(2,128)(2,1)} %copy.39), calls=%async_computation | async-start | bytes 3538944 | tf_op jit(solution)/shard_map/all_to_all | solution.py:70
  35.6 1.4 %copy.61 = bf16[2,1,3,384,384]{4,3,0,2,1:T(8,128)(2,1)} copy(bf16[2,1,3,384,384]{4,3,2,1,0:T(8,128)(2,1)S(1)} %copy-done) | data formatting | bytes 3538944 | tf_op args[5]
  37.0 3.1 %convolution_bitcast_fusion.1 = f32[384,384]{0,1:T(8,128)} fusion(bf16[2,3,384,384]{3,2,0,1:T(8,128)(2,1)} %bitcast.106, bf16[2,384,1152]{2,1,0:T(8,128)(2,1)} %param.10, bf16[384,384]{0,1:T(8,128)(2,1)} %copy-done.2), kind=kOutput, calls=%fused_computation.12 | convolution fusion | flops 453279744 | bytes 2064384 | tf_op jit(solution)/shard_map/krn,kmn->rm/dot_general | solution.py:44
  40.1 2.8 %convolution_bitcast_fusion = f32[384,384]{0,1:T(8,128)} fusion(bf16[2,3,384,384]{3,2,0,1:T(8,128)(2,1)S(1)} %bitcast.107, bf16[2,384,1152]{2,1,0:T(8,128)(2,1)} %param.10, bf16[384,768]{0,1:T(8,128)(2,1)} %copy-done.3), kind=kOutput, calls=%fused_computation.11 | convolution fusion | flops 453279744 | bytes 2064384 | tf_op jit(solution)/shard_map/krn,kmn->rm/dot_general | solution.py:44
  43.0 3.3 %fusion.11 = f32[384,384]{0,1:T(8,128)} fusion(f32[384,384]{0,1:T(8,128)} %convolution_bitcast_fusion, f32[384,384]{0,1:T(8,128)} %convolution_bitcast_fusion.1, bf16[2,3,384,384]{3,2,0,1:T(8,128)(2,1)S(1)} %bitcast.108, bf16[2,384,1152]{2,1,0:T(8,128)(2,1)} %param.10, bf16[384,768]{0,1:T(8,128)(2,1)} %copy-done.4, pred[384]{0:T(512)(128)(4,1)S(1)} %get-tuple-element.9), kind=kOutput, calls=%fused_computation.25 | convolution fusion | flops 453722112 | bytes 3244544 | tf_op jit(solution)/shard_map/krn,kmn->rm/dot_general | solution.py:44
  46.3 2.1 %copy.58 = f32[384,384]{1,0:T(8,128)} copy(f32[384,384]{0,1:T(8,128)} %fusion.11) | data formatting | bytes 1179648
  48.4 72.8 %reduce-scatter.4.cloned.1.call-done = f32[48,384]{1,0:T(8,128)} async-done(((f32[384,384]{1,0:T(8,128)}), f32[48,384]{1,0:T(8,128)}) %reduce-scatter.4.cloned.1.call-update) | async-done | bytes 73744
  121.1 1.0 copy.59
  122.1 0.7 copy.42
  122.9 0.2 copy.40
  123.1 1.3 %copy.41 = bf16[8,2,48,1152]{3,2,1,0:T(8,128)(2,1)} copy(bf16[8,2,48,1152]{3,2,0,1:T(8,128)(2,1)S(1)} %bitcast.104) | data formatting | bytes 3538944 | tf_op jit(solution)/shard_map/all_to_all | solution.py:70
  (14 shorter events, 0.1 us)
Async XLA Ops:
  11.0 0.7 copy-start.2
  11.8 6.4 %collective-permute-start.1 = (bf16[384,768]{0,1:T(8,128)(2,1)S(1)}, bf16[384,768]{0,1:T(8,128)(2,1)S(1)}, u32[]{:S(2)}, u32[]{:S(2)}) collective-permute-start(bf16[384,768]{0,1:T(8,128)(2,1)S(1)} %pad_maximum_fusion.1), channel_id=1, source_target_pairs={{8,0},{16,8},{24,16},{9,1},{17,9},{25,17},{10,2},{18,10},{26,18},{... | collective-permute-start | bytes 1769480 | tf_op jit(solution)/shard_map/ppermute | solution.py:15
  13.1 7.4 %collective-permute-start = (bf16[384,768]{0,1:T(8,128)(2,1)S(1)}, bf16[384,768]{0,1:T(8,128)(2,1)S(1)}, u32[]{:S(2)}, u32[]{:S(2)}) collective-permute-start(bf16[384,768]{0,1:T(8,128)(2,1)S(1)} %pad_maximum_fusion.1), channel_id=1, source_target_pairs={{0,8},{8,16},{16,24},{1,9},{9,17},{17,25},{2,10},{10,18},{18,26},{... | collective-permute-start | bytes 1769480 | tf_op jit(solution)/shard_map/ppermute | solution.py:12
  18.2 2.3 %copy-start.3 = (bf16[384,768]{0,1:T(8,128)(2,1)}, bf16[384,768]{0,1:T(8,128)(2,1)S(1)}, u32[]{:S(2)}) copy-start(bf16[384,768]{0,1:T(8,128)(2,1)S(1)} %collective-permute-done.1) | copy-start | bytes 1769476
  20.5 0.8 copy-start.4
  28.1 7.5 %copy-start = (bf16[2,1,3,384,384]{4,3,2,1,0:T(8,128)(2,1)S(1)}, bf16[2,1,3,384,384]{4,3,2,1,0:T(8,128)(2,1)}, u32[]{:S(2)}) copy-start(bf16[2,1,3,384,384]{4,3,2,1,0:T(8,128)(2,1)} %param.11) | copy-start | bytes 5308420
  28.1 94.8 %all-to-all-start = ((bf16[2,384,1152]{2,0,1:T(2,128)(2,1)}), bf16[2,384,1152]{2,0,1:T(2,128)(2,1)S(1)}, u32[]{:S(2)}, u32[]{:S(2)}) async-start(bf16[2,384,1152]{2,0,1:T(2,128)(2,1)} %copy.39), calls=%async_computation | async-start | bytes 3538944 | tf_op jit(solution)/shard_map/all_to_all | solution.py:70
  35.5 85.6 %reduce-scatter.4.cloned.1.call-start = ((), (), s32[]{:S(2)}) async-start(), calls=%async_computation.2 | async-start | bytes 663552
  37.0 3.1 %copy-start.1 = (bf16[2,1,3,384,384]{4,3,0,2,1:T(8,128)(2,1)S(1)}, bf16[2,1,3,384,384]{4,3,0,2,1:T(8,128)(2,1)}, u32[]{:S(2)}) copy-start(bf16[2,1,3,384,384]{4,3,0,2,1:T(8,128)(2,1)} %copy.61) | copy-start | bytes 5308420
Sparse Core Ops, SparseCore 0:
  48.5 72.5 reduce-scatter.3
where the time goes:
time: 132 us; the launch traced here: 131 us
  waiting for transfers between devices  72.8 us (55%)
  matrix products  15.6 us (12%)
  between operations  15.5 us (12%)
  local copies, waits for them, and re-layouts  15.1 us (11%)
  starting transfers between devices  11.8 us (9%)
    unnamed x2, waiting for transfers between devices  72.8 us
    dot_general x3, matrix products, local(): jnp.einsum('krn,kmn->rm', product, right_part[:, sigma_neighbor], preferr...  9.29 us
    unnamed x16, local copies, waits for them, and re-layouts  9.08 us
    all_to_all x1, starting transfers between devices, local(): lax.all_to_all(renorm_local, 'op', split_axis=1, concat_axis=0, tiled=True)  7.42 us
    dot_general x3, matrix products, renorm_piece(): jnp.einsum('rc,krq->kcq', basis_live, vmatrix, preferred_element_type=jnp...  6.34 us
    concatenate x1, local copies, waits for them, and re-layouts, local(): jnp.concatenate([renorm_piece(neighbor) for neighbor in range(3)], axis=2)  4.47 us
    ppermute x1, starting transfers between devices, padded(): lax.ppermute(lax.slice_in_dim(block, block.shape[dim] - width, None, axis...  3.07 us
  transfers between devices with their start and end apart: 4, of which 1 were waited for; matrix products, arithmetic and copies ran while one was open for 14% of the time, Pallas kernels for 0%

commit v1 on v0

v1 whole, which is shorter than its diff:
```python
import functools

import jax
import jax.numpy as jnp
from jax import lax
from jax.experimental import pallas as pl
from jax.experimental.pallas import tpu as pltpu
from jax.sharding import PartitionSpec as P

MESH = pl.DeviceIdType.MESH


def kernel(
    sec_n, op_n, rows_ref, cols_ref, psi_hbm, basis_hbm, left_hbm, right_hbm,
    sigma_ref, renorm_ref,
    psi_raw, basis_raw, near_psi, near_basis, basis_t, left, right, full, stage,
    total, sigma_stage, sigma_parts,
    load_sem, halo_send, halo_recv, send_sem, recv_sem, sigma_send, sigma_recv,
):
    ops, row_count, _ = left.shape
    kept = basis_raw.shape[1]
    width = psi_raw.shape[1]
    share = stage.shape[2]
    sigma_share = sigma_stage.shape[1]
    sec = lax.axis_index("sec")
    op = lax.axis_index("op")
    has = (sec > 0, None, sec < sec_n - 1)

    loads = [pltpu.make_async_copy(basis_hbm, basis_raw, load_sem.at[0])]
    loads += [pltpu.make_async_copy(left_hbm.at[k], left.at[k], load_sem.at[1 + k]) for k in range(ops)]
    loads += [
        pltpu.make_async_copy(psi_hbm, psi_raw, load_sem.at[1 + ops]),
        pltpu.make_async_copy(right_hbm, right, load_sem.at[2 + ops]),
    ]
    for load in loads:
        load.start()

    barrier = pltpu.get_barrier_semaphore()

    def greet(step, carry):
        pl.semaphore_signal(
            barrier, inc=1, device_id=(sec, lax.rem(op + step, op_n)), device_id_type=MESH
        )
        return carry

    for d in (0, 2):
        @pl.when(has[d])
        def _():
            pl.semaphore_signal(barrier, inc=1, device_id=(sec + d - 1, op), device_id_type=MESH)
    lax.fori_loop(1, op_n, greet, 0)

    live = lax.broadcasted_iota(jnp.int32, (row_count, kept), 0) < rows_ref[0]
    live_kept = live & (lax.broadcasted_iota(jnp.int32, (row_count, kept), 1) < cols_ref[0])
    loads[0].wait()
    masked = jnp.where(live_kept, basis_raw[...].astype(jnp.float32), 0.0)
    near_basis[1] = masked.astype(jnp.bfloat16)
    live_state = lax.broadcasted_iota(jnp.int32, (row_count, width), 0) < rows_ref[0]
    loads[1 + ops].wait()
    near_psi[1] = jnp.where(live_state, psi_raw[...].astype(jnp.float32), 0.0).astype(jnp.bfloat16)

    beside = (sec > 0).astype(jnp.int32) + (sec < sec_n - 1).astype(jnp.int32)
    pl.semaphore_wait(barrier, op_n - 1 + beside)

    def halo(near, at, d):
        return pltpu.make_async_remote_copy(
            src_ref=near.at[1], dst_ref=near.at[2 - d],
            send_sem=halo_send.at[at, d], recv_sem=halo_recv.at[at, 2 - d],
            device_id=(sec + d - 1, op), device_id_type=MESH,
        )

    def arrival(near, at, d):
        return pltpu.make_async_remote_copy(
            src_ref=near.at[1], dst_ref=near.at[d],
            send_sem=halo_send.at[at, d], recv_sem=halo_recv.at[at, d],
            device_id=(sec + d - 1, op), device_id_type=MESH,
        )

    for at, near in ((0, near_basis), (1, near_psi)):
        for d in (0, 2):
            @pl.when(has[d])
            def _():
                halo(near, at, d).start()

    basis_t[...] = masked.T.astype(jnp.bfloat16)

    def piece(k, d, source, slot, peer):
        return pltpu.make_async_remote_copy(
            src_ref=stage.at[k * 3 + d, slot],
            dst_ref=renorm_ref.at[source * ops + k, :, pl.ds(d * kept, kept)],
            send_sem=send_sem.at[k * 3 + d, slot], recv_sem=recv_sem.at[k * 3 + d, source],
            device_id=(sec, peer), device_id_type=MESH,
        )

    def cut(target, value, count, each):
        if each % 16 == 0:
            for p in range(count):
                target[p] = value[p * each : (p + 1) * each].astype(jnp.bfloat16)
        else:
            full[:, : value.shape[1]] = value
            for p in range(count):
                target[p] = full[pl.ds(p * each, each), : value.shape[1]].astype(jnp.bfloat16)

    def renorm(k, d):
        vmatrix = jnp.dot(
            left[k, :, d * row_count : (d + 1) * row_count], near_basis[d],
            preferred_element_type=jnp.float32,
        ).astype(jnp.bfloat16)
        value = jnp.dot(basis_t[...], vmatrix, preferred_element_type=jnp.float32)
        cut(stage.at[k * 3 + d], value, op_n, share)

        def send(step, carry):
            peer = lax.rem(op + step, op_n)
            piece(k, d, op, peer, peer).start()
            return carry

        lax.fori_loop(1, op_n, send, 0)
        renorm_ref[op * ops + k, :, d * kept : (d + 1) * kept] = stage[k * 3 + d, op]

    for k in range(ops):
        loads[1 + k].wait()
        renorm(k, 1)
    for d in (0, 2):
        @pl.when(has[d])
        def _():
            arrival(near_basis, 0, d).wait_recv()
            for k in range(ops):
                renorm(k, d)

        @pl.when(jnp.logical_not(has[d]))
        def _():
            def clear(g, carry):
                renorm_ref[g, :, d * kept : (d + 1) * kept] = jnp.zeros((share, kept), jnp.bfloat16)
                return carry

            lax.fori_loop(0, op_n * ops, clear, 0)

    loads[2 + ops].wait()

    def sigma_term(k, d):
        product = jnp.dot(
            left[k, :, d * row_count : (d + 1) * row_count], near_psi[d],
            preferred_element_type=jnp.float32,
        ).astype(jnp.bfloat16)
        return lax.dot_general(
            product, right[k, d], (((1,), (1,)), ((), ())), preferred_element_type=jnp.float32
        )

    total[...] = sum(sigma_term(k, 1) for k in range(ops))
    for d in (0, 2):
        @pl.when(has[d])
        def _():
            arrival(near_psi, 1, d).wait_recv()
            total[...] += sum(sigma_term(k, d) for k in range(ops))

    cut(sigma_stage, jnp.where(live_state, total[...], 0.0), op_n, sigma_share)

    def sigma_piece(source, slot, peer):
        return pltpu.make_async_remote_copy(
            src_ref=sigma_stage.at[slot], dst_ref=sigma_parts.at[source],
            send_sem=sigma_send.at[slot], recv_sem=sigma_recv.at[source],
            device_id=(sec, peer), device_id_type=MESH,
        )

    def sigma_start(step, carry):
        peer = lax.rem(op + step, op_n)
        sigma_piece(op, peer, peer).start()
        return carry

    lax.fori_loop(1, op_n, sigma_start, 0)
    total[:sigma_share] = sigma_stage[op].astype(jnp.float32)

    def sigma_add(step, carry):
        source = lax.rem(op + op_n - step, op_n)
        sigma_piece(source, source, source).wait_recv()
        total[:sigma_share] += sigma_parts[source].astype(jnp.float32)
        return carry

    lax.fori_loop(1, op_n, sigma_add, 0)
    sigma_ref[...] = total[:sigma_share].astype(jnp.bfloat16)

    def finish(k, d):
        def one(step, carry):
            source = lax.rem(op + op_n - step, op_n)
            piece(k, d, source, source, source).wait()
            return carry

        lax.fori_loop(1, op_n, one, 0)

    for k in range(ops):
        finish(k, 1)
    for d in (0, 2):
        @pl.when(has[d])
        def _():
            halo(near_basis, 0, d).wait_send()
            halo(near_psi, 1, d).wait_send()
            for k in range(ops):
                finish(k, d)

    def sigma_sent(step, carry):
        peer = lax.rem(op + step, op_n)
        sigma_piece(op, peer, peer).wait_send()
        return carry

    lax.fori_loop(1, op_n, sigma_sent, 0)


def local(sec_n, op_n, psi_blocks, sector_rows, kept_cols, basis, left_ops, right_ops):
    row_count, width = psi_blocks.shape
    kept = basis.shape[1]
    ops = left_ops.shape[0]
    share = kept // op_n
    sigma_share = row_count // op_n
    bf16 = jnp.bfloat16
    vmem = pl.BlockSpec(memory_space=pltpu.VMEM)
    smem = pl.BlockSpec(memory_space=pltpu.SMEM)
    hbm = pl.BlockSpec(memory_space=pl.ANY)
    dma = pltpu.SemaphoreType.DMA
    return pl.pallas_call(
        functools.partial(kernel, sec_n, op_n),
        out_shape=(
            jax.ShapeDtypeStruct((sigma_share, width), bf16),
            jax.ShapeDtypeStruct((ops * op_n, share, 3 * kept), bf16),
        ),
        in_specs=[smem, smem, hbm, hbm, hbm, hbm],
        out_specs=(vmem, vmem),
        scratch_shapes=[
            pltpu.VMEM((row_count, width), bf16),
            pltpu.VMEM((row_count, kept), bf16),
            pltpu.VMEM((3, row_count, width), bf16),
            pltpu.VMEM((3, row_count, kept), bf16),
            pltpu.VMEM((kept, row_count), bf16),
            pltpu.VMEM((ops, row_count, 3 * row_count), bf16),
            pltpu.VMEM((ops, 3, width, width), bf16),
            pltpu.VMEM((max(row_count, kept), max(width, kept)), jnp.float32),
            pltpu.VMEM((ops * 3, op_n, share, kept), bf16),
            pltpu.VMEM((row_count, width), jnp.float32),
            pltpu.VMEM((op_n, sigma_share, width), bf16),
            pltpu.VMEM((op_n, sigma_share, width), bf16),
            dma((ops + 3,)),
            dma((2, 3)),
            dma((2, 3)),
            dma((ops * 3, op_n)),
            dma((ops * 3, op_n)),
            dma((op_n,)),
            dma((op_n,)),
        ],
        compiler_params=pltpu.CompilerParams(
            collective_id=0, has_side_effects=True, vmem_limit_bytes=56 * 1024 * 1024
        ),
    )(sector_rows, kept_cols, psi_blocks, basis, left_ops, right_ops[:, 0])


def solution(mesh):
    placed = (
        P("sec", None),
        P("sec"),
        P("sec"),
        P("sec", None),
        P("op", "sec", None),
        P("op", "sec", None, None, None),
    )
    return jax.shard_map(
        functools.partial(local, mesh.shape["sec"], mesh.shape["op"]),
        mesh=mesh,
        in_specs=placed,
        out_specs=(P(("sec", "op"), None), P(None, ("sec", "op"), None)),
        check_vma=False,
    )
```

time: 132 us -> 53.8 us (0.41)
  the two profiles are of different devices: /device:TPU:0 before, /device:TPU:1 now
where the time goes in v1:
time: 53.8 us; the launch traced here: 53.6 us
  Pallas kernels  47.5 us (88%)
  local copies, waits for them, and re-layouts  4.21 us (8%)
  between operations  1.93 us (4%)
    pallas_call x1, Pallas kernels, local(): pl.pallas_call(functools.partial(kernel, sec_n, op_n), out_shape=(jax.Sha...  47.5 us
    unnamed x2, local copies, waits for them, and re-layouts  4.21 us

profile of v1, /device:TPU:1, one launch (start us, length us, event | category | flops | bytes accessed | tf_op | source)
XLA Modules:
  0.0 53.6 jit_solution(16405136633835205784)
XLA Ops:
  1.9 47.5 %shard_map.77 = (bf16[48,384]{1,0:T(8,128)(2,1)}, bf16[16,48,1152]{2,1,0:T(8,128)(2,1)}) custom-call(s32[1]{0:T(128)S(6)} %copy.10.rows_ref, s32[1]{0:T(128)S(6)} %copy.11.cols_ref, bf16[384,384]{1,0:T(8,128)(2,1)} %psi_hbm.1, bf16[384,384]{1,0:T(8,128)(2,1)} %basis_hbm.1, bf16[2,384,1152]{2,1,0:T(8,128)(2,1)} %left_hbm.1, bf16[2,3,384,384]{3,2,1,0:T(8,128)(2,1)} %bitcast.1), custom_call_target="tpu_custom_call" | custom-call | tf_op jit(solution)/shard_map/pallas_call | solution.py:218
  49.4 1.4 %copy.12 = bf16[48,384]{1,0:T(8,128)(2,1)} copy(bf16[48,384]{1,0:T(8,128)(2,1)} %get-tuple-element.4) | data formatting | bytes 73728
  50.8 2.8 %copy.13 = bf16[16,48,1152]{2,1,0:T(8,128)(2,1)} copy(bf16[16,48,1152]{2,1,0:T(8,128)(2,1)} %get-tuple-element.5) | data formatting | bytes 3538944

commit v2 on v1

--- a/solution.py
+++ b/solution.py
@@ -14,14 +14,14 @@
     sec_n, op_n, rows_ref, cols_ref, psi_hbm, basis_hbm, left_hbm, right_hbm,
     sigma_ref, renorm_ref,
     psi_raw, basis_raw, near_psi, near_basis, basis_t, left, right, full, stage,
-    total, sigma_stage, sigma_parts,
+    total, sums, arrived, last,
     load_sem, halo_send, halo_recv, send_sem, recv_sem, sigma_send, sigma_recv,
 ):
     ops, row_count, _ = left.shape
     kept = basis_raw.shape[1]
     width = psi_raw.shape[1]
     share = stage.shape[2]
-    sigma_share = sigma_stage.shape[1]
+    sigma_share = sums.shape[1]
     sec = lax.axis_index("sec")
     op = lax.axis_index("op")
     has = (sec > 0, None, sec < sec_n - 1)
@@ -94,11 +94,11 @@
     def cut(target, value, count, each):
         if each % 16 == 0:
             for p in range(count):
-                target[p] = value[p * each : (p + 1) * each].astype(jnp.bfloat16)
+                target[p] = value[p * each : (p + 1) * each].astype(target.dtype)
         else:
             full[:, : value.shape[1]] = value
             for p in range(count):
-                target[p] = full[pl.ds(p * each, each), : value.shape[1]].astype(jnp.bfloat16)
+                target[p] = full[pl.ds(p * each, each), : value.shape[1]].astype(target.dtype)
 
     def renorm(k, d):
         vmatrix = jnp.dot(
@@ -119,7 +119,7 @@
     for k in range(ops):
         loads[1 + k].wait()
         renorm(k, 1)
-    for d in (0, 2):
+    def side(d):
         @pl.when(has[d])
         def _():
             arrival(near_basis, 0, d).wait_recv()
@@ -152,31 +152,54 @@
             arrival(near_psi, 1, d).wait_recv()
             total[...] += sum(sigma_term(k, d) for k in range(ops))
 
-    cut(sigma_stage, jnp.where(live_state, total[...], 0.0), op_n, sigma_share)
-
-    def sigma_piece(source, slot, peer):
-        return pltpu.make_async_remote_copy(
-            src_ref=sigma_stage.at[slot], dst_ref=sigma_parts.at[source],
-            send_sem=sigma_send.at[slot], recv_sem=sigma_recv.at[source],
-            device_id=(sec, peer), device_id_type=MESH,
-        )
-
-    def sigma_start(step, carry):
-        peer = lax.rem(op + step, op_n)
-        sigma_piece(op, peer, peer).start()
-        return carry
-
-    lax.fori_loop(1, op_n, sigma_start, 0)
-    total[:sigma_share] = sigma_stage[op].astype(jnp.float32)
-
-    def sigma_add(step, carry):
-        source = lax.rem(op + op_n - step, op_n)
-        sigma_piece(source, source, source).wait_recv()
-        total[:sigma_share] += sigma_parts[source].astype(jnp.float32)
-        return carry
-
-    lax.fori_loop(1, op_n, sigma_add, 0)
-    sigma_ref[...] = total[:sigma_share].astype(jnp.bfloat16)
+    cut(sums, jnp.where(live_state, total[...], 0.0), op_n, sigma_share)
+
+    levels = op_n.bit_length() - 1
+
+    def partner(level):
+        return op + (1 - 2 * (op // 2**level % 2)) * 2**level
+
+    def sigma_piece(level, j, mine):
+        low = op % 2**level
+        here, there = op // 2**level % 2, partner(level) // 2**level % 2
+        owner = low + (here if mine else there) * 2**level + j * 2 ** (level + 1)
+        slot = op_n - op_n // 2**level + j
+        if level == levels - 1:
+            source, target = last.at[0], last.at[1]
+        else:
+            source, target = sums.at[owner], arrived.at[slot]
+        return owner, pltpu.make_async_remote_copy(
+            src_ref=source, dst_ref=target,
+            send_sem=sigma_send.at[slot], recv_sem=sigma_recv.at[slot],
+            device_id=(sec, partner(level)), device_id_type=MESH,
+        )
+
+    def sigma_start(level):
+        for j in range(op_n // 2 ** (level + 1)):
+            owner, copy = sigma_piece(level, j, False)
+            if level == levels - 1:
+                last[0] = sums[owner].astype(jnp.bfloat16)
+            copy.start()
+
+    def sigma_add(level):
+        for j in range(op_n // 2 ** (level + 1)):
+            owner, copy = sigma_piece(level, j, True)
+            copy.wait_recv()
+            slot = op_n - op_n // 2**level + j
+            if level == levels - 1:
+                sigma_ref[...] = (sums[owner] + last[1].astype(jnp.float32)).astype(jnp.bfloat16)
+            else:
+                sums[owner] += arrived[slot]
+
+    sigma_start(0)
+    side(0)
+    sigma_add(0)
+    sigma_start(1)
+    side(2)
+    for level in range(1, levels):
+        sigma_add(level)
+        if level + 1 < levels:
+            sigma_start(level + 1)
 
     def finish(k, d):
         def one(step, carry):
@@ -196,12 +219,9 @@
             for k in range(ops):
                 finish(k, d)
 
-    def sigma_sent(step, carry):
-        peer = lax.rem(op + step, op_n)
-        sigma_piece(op, peer, peer).wait_send()
-        return carry
-
-    lax.fori_loop(1, op_n, sigma_sent, 0)
+    for level in range(levels):
+        for j in range(op_n // 2 ** (level + 1)):
+            sigma_piece(level, j, False)[1].wait_send()
 
 
 def local(sec_n, op_n, psi_blocks, sector_rows, kept_cols, basis, left_ops, right_ops):
@@ -234,8 +254,9 @@
             pltpu.VMEM((max(row_count, kept), max(width, kept)), jnp.float32),
             pltpu.VMEM((ops * 3, op_n, share, kept), bf16),
             pltpu.VMEM((row_count, width), jnp.float32),
-            pltpu.VMEM((op_n, sigma_share, width), bf16),
-            pltpu.VMEM((op_n, sigma_share, width), bf16),
+            pltpu.VMEM((op_n, sigma_share, width), jnp.float32),
+            pltpu.VMEM((op_n, sigma_share, width), jnp.float32),
+            pltpu.VMEM((2, sigma_share, width), bf16),
             dma((ops + 3,)),
             dma((2, 3)),
             dma((2, 3)),

time: 53.8 us -> 49.9 us (0.928)
  Pallas kernels: 47.5 us -> 43.5 us
    pallas_call x1, Pallas kernels: 47.5 us -> 43.5 us  [local(): pl.pallas_call(functools.partial(kernel, sec_n, op_n), out_shape=(jax.Sha...]
where the time goes in v2:
time: 49.9 us; the launch traced here: 49.6 us
  Pallas kernels  43.5 us (87%)
  local copies, waits for them, and re-layouts  4.21 us (8%)
  between operations  1.93 us (4%)
    pallas_call x1, Pallas kernels, local(): pl.pallas_call(functools.partial(kernel, sec_n, op_n), out_shape=(jax.Sha...  43.5 us
    unnamed x2, local copies, waits for them, and re-layouts  4.21 us

profile of v2, /device:TPU:1, one launch (start us, length us, event | category | flops | bytes accessed | tf_op | source)
XLA Modules:
  0.0 49.6 jit_solution(267247927771305790)
XLA Ops:
  1.9 43.5 %shard_map.77 = (bf16[48,384]{1,0:T(8,128)(2,1)}, bf16[16,48,1152]{2,1,0:T(8,128)(2,1)}) custom-call(s32[1]{0:T(128)S(6)} %copy.10.rows_ref, s32[1]{0:T(128)S(6)} %copy.11.cols_ref, bf16[384,384]{1,0:T(8,128)(2,1)} %psi_hbm.1, bf16[384,384]{1,0:T(8,128)(2,1)} %basis_hbm.1, bf16[2,384,1152]{2,1,0:T(8,128)(2,1)} %left_hbm.1, bf16[2,3,384,384]{3,2,1,0:T(8,128)(2,1)} %bitcast.1), custom_call_target="tpu_custom_call" | custom-call | tf_op jit(solution)/shard_map/pallas_call | solution.py:238
  45.4 1.4 %copy.12 = bf16[48,384]{1,0:T(8,128)(2,1)} copy(bf16[48,384]{1,0:T(8,128)(2,1)} %get-tuple-element.4) | data formatting | bytes 73728
  46.8 2.8 %copy.13 = bf16[16,48,1152]{2,1,0:T(8,128)(2,1)} copy(bf16[16,48,1152]{2,1,0:T(8,128)(2,1)} %get-tuple-element.5) | data formatting | bytes 3538944

commit v3 on v2

--- a/solution.py
+++ b/solution.py
@@ -224,6 +224,17 @@
             sigma_piece(level, j, False)[1].wait_send()
 
 
+def deliver(sigma_in, renorm_in, sigma_out, renorm_out, sem):
+    copies = (
+        pltpu.make_async_copy(sigma_in, sigma_out, sem.at[0]),
+        pltpu.make_async_copy(renorm_in, renorm_out, sem.at[1]),
+    )
+    for copy in copies:
+        copy.start()
+    for copy in copies:
+        copy.wait()
+
+
 def local(sec_n, op_n, psi_blocks, sector_rows, kept_cols, basis, left_ops, right_ops):
     row_count, width = psi_blocks.shape
     kept = basis.shape[1]
@@ -235,12 +246,13 @@
     smem = pl.BlockSpec(memory_space=pltpu.SMEM)
     hbm = pl.BlockSpec(memory_space=pl.ANY)
     dma = pltpu.SemaphoreType.DMA
-    return pl.pallas_call(
+    results = (
+        jax.ShapeDtypeStruct((sigma_share, width), bf16),
+        jax.ShapeDtypeStruct((ops * op_n, share, 3 * kept), bf16),
+    )
+    made = pl.pallas_call(
         functools.partial(kernel, sec_n, op_n),
-        out_shape=(
-            jax.ShapeDtypeStruct((sigma_share, width), bf16),
-            jax.ShapeDtypeStruct((ops * op_n, share, 3 * kept), bf16),
-        ),
+        out_shape=tuple(pltpu.VMEM(x.shape, x.dtype) for x in results),
         in_specs=[smem, smem, hbm, hbm, hbm, hbm],
         out_specs=(vmem, vmem),
         scratch_shapes=[
@@ -269,6 +281,14 @@
             collective_id=0, has_side_effects=True, vmem_limit_bytes=56 * 1024 * 1024
         ),
     )(sector_rows, kept_cols, psi_blocks, basis, left_ops, right_ops[:, 0])
+    return pl.pallas_call(
+        deliver,
+        out_shape=results,
+        in_specs=[hbm, hbm],
+        out_specs=(hbm, hbm),
+        scratch_shapes=[dma((2,))],
+        compiler_params=pltpu.CompilerParams(vmem_limit_bytes=1024 * 1024),
+    )(*made)
 
 
 def solution(mesh):

time: 49.9 us -> 45.6 us (0.914)
  local copies, waits for them, and re-layouts: 4.21 us -> 0 us
    unnamed x2 -> x0, local copies, waits for them, and re-layouts: 4.21 us -> none
    pallas_call x1 -> x2, Pallas kernels: 43.5 us -> 43.5 us  [the longest x1 42.2 us: local(): pl.pallas_call(functools.partial(kernel, sec_n, op_n), out_shape=tuple((p...]
where the time goes in v3:
time: 45.6 us; the launch traced here: 45.4 us
  Pallas kernels  43.5 us (95%)
  between operations  1.93 us (4%)
    pallas_call x1, Pallas kernels, local(): pl.pallas_call(functools.partial(kernel, sec_n, op_n), out_shape=tuple((p...  42.2 us
    pallas_call x1, Pallas kernels, local(): pl.pallas_call(deliver, out_shape=results, in_specs=[hbm, hbm], out_specs...  1.24 us

profile of v3, /device:TPU:1, one launch (start us, length us, event | category | flops | bytes accessed | tf_op | source)
XLA Modules:
  0.0 45.4 jit_solution(3922213290021272811)
XLA Ops:
  1.9 42.2 %shard_map.77 = (bf16[48,384]{1,0:T(8,128)(2,1)S(1)}, bf16[16,48,1152]{2,1,0:T(8,128)(2,1)S(1)}) custom-call(s32[1]{0:T(128)S(6)} %copy.8.rows_ref, s32[1]{0:T(128)S(6)} %copy.9.cols_ref, bf16[384,384]{1,0:T(8,128)(2,1)} %psi_hbm.1, bf16[384,384]{1,0:T(8,128)(2,1)} %basis_hbm.1, bf16[2,384,1152]{2,1,0:T(8,128)(2,1)} %left_hbm.1, bf16[2,3,384,384]{3,2,1,0:T(8,128)(2,1)} %bitcast.1), custom_call_target="tpu_custom_call" | custom-call | tf_op jit(solution)/shard_map/pallas_call | solution.py:253
  44.2 1.2 %shard_map.78 = (bf16[48,384]{1,0:T(8,128)(2,1)}, bf16[16,48,1152]{2,1,0:T(8,128)(2,1)}) custom-call(bf16[48,384]{1,0:T(8,128)(2,1)S(1)} %get-tuple-element.4.sigma_in, bf16[16,48,1152]{2,1,0:T(8,128)(2,1)S(1)} %get-tuple-element.5.renorm_in), custom_call_target="tpu_custom_call" | custom-call | tf_op jit(solution)/shard_map/pallas_call | solution.py:284

commit v4 on v3

--- a/solution.py
+++ b/solution.py
@@ -109,7 +109,7 @@
         cut(stage.at[k * 3 + d], value, op_n, share)
 
         def send(step, carry):
-            peer = lax.rem(op + step, op_n)
+            peer = lax.rem(op + 1 + lax.rem(step - 1 + op, op_n - 1), op_n)
             piece(k, d, op, peer, peer).start()
             return carry
 

time: 45.6 us -> 45.5 us (level)
  no operation moved by 1% of the time
where the time goes in v4:
time: 45.5 us; the launch traced here: 45.3 us
  Pallas kernels  43.4 us (95%)
  between operations  1.93 us (4%)
    pallas_call x1, Pallas kernels, local(): pl.pallas_call(functools.partial(kernel, sec_n, op_n), out_shape=tuple((p...  42.2 us
    pallas_call x1, Pallas kernels, local(): pl.pallas_call(deliver, out_shape=results, in_specs=[hbm, hbm], out_specs...  1.24 us

profile of v4, /device:TPU:1, one launch (start us, length us, event | category | flops | bytes accessed | tf_op | source)
XLA Modules:
  0.0 45.3 jit_solution(211801597409606310)
XLA Ops:
  1.9 42.2 %shard_map.77 = (bf16[48,384]{1,0:T(8,128)(2,1)S(1)}, bf16[16,48,1152]{2,1,0:T(8,128)(2,1)S(1)}) custom-call(s32[1]{0:T(128)S(6)} %copy.8.rows_ref, s32[1]{0:T(128)S(6)} %copy.9.cols_ref, bf16[384,384]{1,0:T(8,128)(2,1)} %psi_hbm.1, bf16[384,384]{1,0:T(8,128)(2,1)} %basis_hbm.1, bf16[2,384,1152]{2,1,0:T(8,128)(2,1)} %left_hbm.1, bf16[2,3,384,384]{3,2,1,0:T(8,128)(2,1)} %bitcast.1), custom_call_target="tpu_custom_call" | custom-call | tf_op jit(solution)/shard_map/pallas_call | solution.py:253
  44.1 1.2 %shard_map.78 = (bf16[48,384]{1,0:T(8,128)(2,1)}, bf16[16,48,1152]{2,1,0:T(8,128)(2,1)}) custom-call(bf16[48,384]{1,0:T(8,128)(2,1)S(1)} %get-tuple-element.4.sigma_in, bf16[16,48,1152]{2,1,0:T(8,128)(2,1)S(1)} %get-tuple-element.5.renorm_in), custom_call_target="tpu_custom_call" | custom-call | tf_op jit(solution)/shard_map/pallas_call | solution.py:284

commit v5 on v4

--- a/solution.py
+++ b/solution.py
@@ -75,7 +75,7 @@
             device_id=(sec + d - 1, op), device_id_type=MESH,
         )
 
-    for at, near in ((0, near_basis), (1, near_psi)):
+    def halos(near, at):
         for d in (0, 2):
             @pl.when(has[d])
             def _():
@@ -119,6 +119,10 @@
     for k in range(ops):
         loads[1 + k].wait()
         renorm(k, 1)
+        if k == 0:
+            halos(near_basis, 0)
+    halos(near_psi, 1)
+
     def side(d):
         @pl.when(has[d])
         def _():
@@ -134,6 +138,8 @@
 
             lax.fori_loop(0, op_n * ops, clear, 0)
 
+    side(0)
+    side(2)
     loads[2 + ops].wait()
 
     def sigma_term(k, d):
@@ -192,10 +198,8 @@
                 sums[owner] += arrived[slot]
 
     sigma_start(0)
-    side(0)
     sigma_add(0)
     sigma_start(1)
-    side(2)
     for level in range(1, levels):
         sigma_add(level)
         if level + 1 < levels:

time: 45.5 us -> 45.4 us (level)
  no operation moved by 1% of the time
where the time goes in v5:
time: 45.4 us; the launch traced here: 45.3 us
  Pallas kernels  43.4 us (96%)
  between operations  1.93 us (4%)
    pallas_call x1, Pallas kernels, local(): pl.pallas_call(functools.partial(kernel, sec_n, op_n), out_shape=tuple((p...  42.1 us
    pallas_call x1, Pallas kernels, local(): pl.pallas_call(deliver, out_shape=results, in_specs=[hbm, hbm], out_specs...  1.24 us

profile of v5, /device:TPU:1, one launch (start us, length us, event | category | flops | bytes accessed | tf_op | source)
XLA Modules:
  0.0 45.3 jit_solution(7483688879545873269)
XLA Ops:
  1.9 42.1 %shard_map.77 = (bf16[48,384]{1,0:T(8,128)(2,1)S(1)}, bf16[16,48,1152]{2,1,0:T(8,128)(2,1)S(1)}) custom-call(s32[1]{0:T(128)S(6)} %copy.8.rows_ref, s32[1]{0:T(128)S(6)} %copy.9.cols_ref, bf16[384,384]{1,0:T(8,128)(2,1)} %psi_hbm.1, bf16[384,384]{1,0:T(8,128)(2,1)} %basis_hbm.1, bf16[2,384,1152]{2,1,0:T(8,128)(2,1)} %left_hbm.1, bf16[2,3,384,384]{3,2,1,0:T(8,128)(2,1)} %bitcast.1), custom_call_target="tpu_custom_call" | custom-call | tf_op jit(solution)/shard_map/pallas_call | solution.py:257
  44.1 1.2 %shard_map.78 = (bf16[48,384]{1,0:T(8,128)(2,1)}, bf16[16,48,1152]{2,1,0:T(8,128)(2,1)}) custom-call(bf16[48,384]{1,0:T(8,128)(2,1)S(1)} %get-tuple-element.4.sigma_in, bf16[16,48,1152]{2,1,0:T(8,128)(2,1)S(1)} %get-tuple-element.5.renorm_in), custom_call_target="tpu_custom_call" | custom-call | tf_op jit(solution)/shard_map/pallas_call | solution.py:288
